TPU v7x, 32 devices: a whole 2x2x4 slice. The times are simulated.
32 devices in a mesh: band: 8 (over z, core), grid: 4 (over y, x).
Axes of the slice: x: 2, y: 2, z: 4, core: 2. Of those that a mesh axis runs over, the one named last changes fastest.
Arguments:
- orbitals: float32 [8, 128, 128, 128], P('band', 'grid'), may hold values from -6 to 6
Outputs:
- exchange_field: float32 [8, 128, 128, 128], P('band', 'grid')
All inputs are finite; a program needn't handle non-finite values.
Results may differ from a plain program's by a relative error of at most 0.0001.
Values sent between devices are 32-bit elements; how exact they have to be, the bound alone decides.
A program may use at most 128 MiB of HBM per device.

v0:
```python
import functools
import math

import jax
import jax.numpy as jnp
import numpy as np
from jax import lax
from jax.experimental import pallas as pl
from jax.experimental.pallas import tpu as pltpu
from jax.sharding import PartitionSpec as P

coulomb_scale = 64.0
MESH = pl.DeviceIdType.MESH


def tables(length):
    indices = np.arange(length)
    angles = (indices[:, None] * indices[None, :] % length) * (2.0 * math.pi / length)
    cosine, sine = np.cos(angles), np.sin(angles)
    matrix = np.block([[cosine, -sine], [sine, cosine]]).astype(np.float32)
    lead = matrix.astype(jnp.bfloat16)
    rest = (matrix - lead.astype(np.float32)).astype(jnp.bfloat16)
    return lead, rest, lead.T.copy(), rest.T.copy()


def parts(value):
    lead = value.astype(jnp.bfloat16)
    return lead, (value - lead.astype(jnp.float32)).astype(jnp.bfloat16)


def dot(left, right):
    return jnp.dot(left, right, preferred_element_type=jnp.float32)


def times_table(value, lead, rest):
    value_lead, value_rest = parts(value)
    return dot(value_lead, lead) + (dot(value_rest, lead) + dot(value_lead, rest))


def table_times(lead, rest, value):
    value_lead, value_rest = parts(value)
    return dot(lead, value_lead) + (dot(lead, value_rest) + dot(rest, value_lead))


def kernel(
    bands, peers, planes,
    orb, m_lead, m_rest, t_lead, t_rest, out,
    near, far, send, recv, back, home, far_sum, far_got, near_sum, near_got,
    near_s, near_r, far_s, far_r, fwd_s, fwd_r, bwd_s, bwd_r, cfar_s, cfar_r, cnear_s, cnear_r,
):
    local_x, width_y, width_z = orb.shape
    width_x = local_x * peers
    local_y = width_y // peers
    chunks = local_x // planes
    rows = planes * local_y
    me = lax.axis_index("grid")
    block = lax.axis_index("band")
    ahead = lax.rem(block + 1, bands)
    behind = lax.rem(block + bands - 1, bands)

    def to_band(src, dst, chunk, send_sem, recv_sem, target):
        span = pl.ds(chunk * planes, planes)
        return pltpu.make_async_remote_copy(
            src_ref=src.at[span], dst_ref=dst.at[span],
            send_sem=send_sem.at[chunk], recv_sem=recv_sem.at[chunk],
            device_id=(target, me), device_id_type=MESH,
        )

    def near_copy(c):
        return to_band(orb, near, c, near_s, near_r, ahead)

    def far_copy(c):
        return to_band(near, far, c, far_s, far_r, ahead)

    def far_carry(c):
        return to_band(far_sum, far_got, c, cfar_s, cfar_r, behind)

    def near_carry(c):
        return to_band(near_sum, near_got, c, cnear_s, cnear_r, behind)

    def forward(c, d):
        target = lax.rem(me + d, peers)
        return pltpu.make_async_remote_copy(
            src_ref=send.at[:, target, pl.ds(c * rows, rows), :],
            dst_ref=recv.at[:, pl.ds((me * local_x + c * planes) * local_y, rows), :],
            send_sem=fwd_s.at[c, d - 1], recv_sem=fwd_r.at[c, d - 1],
            device_id=(block, target), device_id_type=MESH,
        )

    def backward(c, d):
        target = lax.rem(me + d, peers)
        return pltpu.make_async_remote_copy(
            src_ref=back.at[:, pl.ds((target * local_x + c * planes) * local_y, rows), :],
            dst_ref=home.at[:, me, pl.ds(c * rows, rows), :],
            send_sem=bwd_s.at[c, d - 1], recv_sem=bwd_r.at[c, d - 1],
            device_id=(block, target), device_id_type=MESH,
        )

    barrier = pltpu.get_barrier_semaphore()
    pl.semaphore_signal(barrier, inc=1, device_id=(ahead, me), device_id_type=MESH)
    pl.semaphore_signal(barrier, inc=1, device_id=(behind, me), device_id_type=MESH)
    for d in range(1, peers):
        pl.semaphore_signal(
            barrier, inc=1, device_id=(block, lax.rem(me + d, peers)), device_id_type=MESH
        )
    pl.semaphore_wait(barrier, peers + 1)

    lead_start = min(2, chunks)
    for c in range(lead_start):
        near_copy(c).start()

    def transform_chunk(c):
        span = pl.ds(c * planes, planes)
        own = orb[span]
        real = (own * near[span]).reshape(planes * width_y, width_z)
        imag = (own * far[span]).reshape(planes * width_y, width_z)
        both = times_table(
            jnp.concatenate([real, imag], axis=1), m_lead[...], m_rest[...]
        )
        stacked = jnp.concatenate(
            [
                jnp.concatenate(
                    [
                        both[p * width_y : (p + 1) * width_y, :width_z],
                        both[p * width_y : (p + 1) * width_y, width_z:],
                    ],
                    axis=0,
                )
                for p in range(planes)
            ],
            axis=1,
        )
        result = table_times(t_lead[...], t_rest[...], stacked)
        for p in range(planes):
            for part in range(2):
                for g in range(peers):
                    at = part * width_y + g * local_y
                    send[part, g, pl.ds(c * rows + p * local_y, local_y), :] = result[
                        at : at + local_y, p * width_z : (p + 1) * width_z
                    ]
        for part in range(2):
            recv[part, pl.ds((me * local_x + c * planes) * local_y, rows), :] = send[
                part, me, pl.ds(c * rows, rows), :
            ]

    def inbound(s, carry):
        @pl.when(s < chunks)
        def _():
            near_copy(s).wait_recv()
            far_copy(s).start()

            @pl.when(s + lead_start < chunks)
            def _():
                near_copy(s + lead_start).start()

        @pl.when(s > 0)
        def _():
            c = s - 1
            far_copy(c).wait_recv()
            transform_chunk(c)
            for d in range(1, peers):
                forward(c, d).start()

        return carry

    lax.fori_loop(0, chunks + 1, inbound, 0)

    def arrived(c, carry):
        for d in range(1, peers):
            forward(c, d).wait_recv()
        return carry

    lax.fori_loop(0, chunks, arrived, 0)

    def signed(index, length):
        return jnp.where(index < length // 2, index, index - length).astype(jnp.float32)

    freq_x = signed(lax.broadcasted_iota(jnp.int32, (width_x, width_z), 0), width_x)
    freq_z = signed(lax.broadcasted_iota(jnp.int32, (width_x, width_z), 1), width_z)
    square_xz = freq_x * freq_x + freq_z * freq_z
    scale = coulomb_scale / float(width_x * width_y * width_z)
    group = 2

    def columns(s, carry):
        loaded = []
        weights = []
        for u in range(group):
            j = s * group + u
            line = pl.ds(j, width_x, stride=local_y)
            loaded.append(jnp.concatenate([recv[0, line, :], recv[1, line, :]], axis=0))
            freq_y = signed(me * local_y + j, width_y)
            square = square_xz + freq_y * freq_y
            weight = jnp.where(square > 0, scale / jnp.maximum(square, 1.0), 0.0)
            weights.append(jnp.concatenate([weight, weight], axis=0))
        field = table_times(t_lead[...], t_rest[...], jnp.concatenate(loaded, axis=1))
        field = field * jnp.concatenate(weights, axis=1)
        field = table_times(m_lead[...], m_rest[...], field)
        for u in range(group):
            line = pl.ds(s * group + u, width_x, stride=local_y)
            for part in range(2):
                back[part, line, :] = field[
                    part * width_x : (part + 1) * width_x, u * width_z : (u + 1) * width_z
                ]
        return carry

    lax.fori_loop(0, local_y // group, columns, 0)

    def send_back(c, carry):
        for d in range(1, peers):
            backward(c, d).start()
        for part in range(2):
            home[part, me, pl.ds(c * rows, rows), :] = back[
                part, pl.ds((me * local_x + c * planes) * local_y, rows), :
            ]
        return carry

    lax.fori_loop(0, chunks, send_back, 0)

    def apply_chunk(c):
        span = pl.ds(c * planes, planes)
        stacked = jnp.concatenate(
            [
                jnp.concatenate(
                    [
                        home[part, g, pl.ds(c * rows + p * local_y, local_y), :]
                        for part in range(2)
                        for g in range(peers)
                    ],
                    axis=0,
                )
                for p in range(planes)
            ],
            axis=1,
        )
        both = table_times(m_lead[...], m_rest[...], stacked)
        joined = jnp.concatenate(
            [
                jnp.concatenate(
                    [
                        both[:width_y, p * width_z : (p + 1) * width_z],
                        both[width_y:, p * width_z : (p + 1) * width_z],
                    ],
                    axis=1,
                )
                for p in range(planes)
            ],
            axis=0,
        )
        both = times_table(joined, t_lead[...], t_rest[...])
        near_pot = both[:, :width_z].reshape(planes, width_y, width_z)
        far_pot = both[:, width_z:].reshape(planes, width_y, width_z)
        own = orb[span]
        far_sum[span] = far_pot * own
        near_sum[span] = near_pot * own
        out[span] = -(near_pot * near[span] + far_pot * far[span])

    def outbound(s, carry):
        @pl.when(s < chunks)
        def _():
            for d in range(1, peers):
                backward(s, d).wait_recv()
            apply_chunk(s)
            far_carry(s).start()

        @pl.when((s > 0) & (s <= chunks))
        def _():
            c = s - 1
            span = pl.ds(c * planes, planes)
            far_carry(c).wait_recv()
            near_sum[span] = near_sum[span] + far_got[span]
            near_carry(c).start()

        @pl.when(s > 1)
        def _():
            c = s - 2
            span = pl.ds(c * planes, planes)
            near_carry(c).wait_recv()
            out[span] = out[span] - near_got[span]

        return carry

    lax.fori_loop(0, chunks + 2, outbound, 0)

    def drain(c, carry):
        near_copy(c).wait_send()
        far_copy(c).wait_send()
        far_carry(c).wait_send()
        near_carry(c).wait_send()
        for d in range(1, peers):
            forward(c, d).wait_send()
            backward(c, d).wait_send()
        return carry

    lax.fori_loop(0, chunks, drain, 0)


def per_device(bands, peers, orbitals):
    _, local_x, width_y, width_z = orbitals.shape
    width_x = local_x * peers
    local_y = width_y // peers
    planes = math.gcd(4, local_x)
    chunks = local_x // planes
    slab = pltpu.VMEM((local_x, width_y, width_z), jnp.float32)
    by_peer = pltpu.VMEM((2, peers, local_x * local_y, width_z), jnp.float32)
    by_line = pltpu.VMEM((2, width_x * local_y, width_z), jnp.float32)
    dma = pltpu.SemaphoreType.DMA
    result = pl.pallas_call(
        functools.partial(kernel, bands, peers, planes),
        out_shape=jax.ShapeDtypeStruct((local_x, width_y, width_z), jnp.float32),
        in_specs=[pl.BlockSpec(memory_space=pltpu.VMEM)] * 5,
        out_specs=pl.BlockSpec(memory_space=pltpu.VMEM),
        scratch_shapes=[slab, slab, by_peer, by_line, by_line, by_peer, slab, slab, slab, slab]
        + [dma((chunks,))] * 4
        + [dma((chunks, peers - 1))] * 4
        + [dma((chunks,))] * 4,
        compiler_params=pltpu.CompilerParams(
            collective_id=0, has_side_effects=True, vmem_limit_bytes=52 * 2**20
        ),
        name="exchange",
    )(orbitals[0], *tables(width_z))
    return result[None]


def solution(mesh):
    spec = P("band", "grid", None, None)
    body = functools.partial(per_device, mesh.shape["band"], mesh.shape["grid"])
    return jax.shard_map(body, mesh=mesh, in_specs=(spec,), out_specs=spec, check_vma=False)
```

profile of v0, /device:TPU:0, one launch (start us, length us, event | category | flops | bytes accessed | tf_op | source)
XLA Modules:
  0.0 143.9 jit_solution(9179588042791284740)
XLA Ops:
  0.0 0.0 copy-start
  0.0 0.9 copy-done
  0.9 0.0 copy-start.1
  0.9 0.9 copy-done.1
  1.8 0.0 copy-start.2
  1.8 0.9 copy-done.2
  2.7 0.0 copy-start.3
  2.7 0.9 copy-done.3
  3.6 137.2 %exchange.1 = f32[32,128,128]{2,1,0:T(8,128)} custom-call(f32[32,128,128]{2,1,0:T(8,128)} %bitcast.3, bf16[256,256]{1,0:T(8,128)(2,1)S(1)} %copy-done.3, bf16[256,256]{1,0:T(8,128)(2,1)S(1)} %copy-done.2, bf16[256,256]{1,0:T(8,128)(2,1)S(1)} %copy-done.1, bf16[256,256]{1,0:T(8,128)(2,1)S(1)} %copy-done), custom_call_target="tpu_custom_call" | custom-call | tf_op jit(solution)/shard_map/exchange/pallas_call | solution.py:307
  140.8 3.1 %copy.7 = f32[1,32,128,128]{3,2,1,0:T(8,128)} copy(f32[1,32,128,128]{3,2,1,0:T(8,128)} %bitcast.2) | data formatting | bytes 4194304
Async XLA Ops:
  0.0 0.9 copy-start
  0.9 0.9 copy-start.1
  1.8 0.9 copy-start.2
  2.7 0.9 copy-start.3
where the time goes:
time: 144 us
  Pallas kernels  137 us (95%)
  local copies, waits for them, and re-layouts  6.75 us (5%)
    pallas_call x1, Pallas kernels, per_device(): pl.pallas_call(functools.partial(kernel, bands, peers, planes), out_shape...  137 us
    unnamed x9, local copies, waits for them, and re-layouts  6.75 us

commit v1 on v0

v1 whole, which is shorter than its diff:
```python
import functools
import math

import jax
import jax.numpy as jnp
import numpy as np
from jax import lax
from jax.experimental import pallas as pl
from jax.experimental.pallas import tpu as pltpu
from jax.sharding import PartitionSpec as P

coulomb_scale = 64.0
MESH = pl.DeviceIdType.MESH


def table(length):
    indices = np.arange(length)
    angles = (indices[:, None] * indices[None, :] % length) * (2.0 * math.pi / length)
    matrix = (np.cos(angles) + np.sin(angles)).astype(np.float32)
    lead = matrix.astype(jnp.bfloat16)
    rest = (matrix - lead.astype(np.float32)).astype(jnp.bfloat16)
    return np.block([[lead, rest], [lead, rest], [lead, lead]])


def parts(value):
    lead = value.astype(jnp.bfloat16)
    return lead, (value - lead.astype(jnp.float32)).astype(jnp.bfloat16)


def dot(left, right):
    return jnp.dot(left, right, preferred_element_type=jnp.float32)


def kernel(
    bands, peers, planes,
    orb_hbm, tab_hbm, out,
    orb, tab, weight, near, far, sends, recvs, backs, homes, far_sum, far_got, near_sum, near_got,
    in_s, near_s, near_r, far_s, far_r, cfar_s, cfar_r, cnear_s, cnear_r, fwd_s, fwd_r, bwd_s, bwd_r,
):
    local_x, width_y, width_z = orb.shape
    width_x = local_x * peers
    local_y = width_y // peers
    chunks = local_x // planes
    rows = planes * local_y
    half = chunks // 2
    me = lax.axis_index("grid")
    block = lax.axis_index("band")
    ahead = lax.rem(block + 1, bands)
    behind = lax.rem(block + bands - 1, bands)

    orb_in = pltpu.make_async_copy(orb_hbm, orb, in_s.at[0])
    tab_in = pltpu.make_async_copy(tab_hbm, tab, in_s.at[1])
    orb_in.start()
    tab_in.start()

    def to_band(src, dst, chunk, send_sem, recv_sem, target):
        span = pl.ds(chunk * planes, planes)
        return pltpu.make_async_remote_copy(
            src_ref=src.at[span], dst_ref=dst.at[span],
            send_sem=send_sem.at[chunk], recv_sem=recv_sem.at[chunk],
            device_id=(target, me), device_id_type=MESH,
        )

    def near_copy(c):
        return to_band(orb, near, c, near_s, near_r, ahead)

    def far_copy(c):
        return to_band(near, far, c, far_s, far_r, ahead)

    def far_carry(c):
        return to_band(far_sum, far_got, c, cfar_s, cfar_r, behind)

    def near_carry(c):
        return to_band(near_sum, near_got, c, cnear_s, cnear_r, behind)

    def own_lines(c):
        return pl.ds((me * local_x + c * planes) * local_y, rows)

    def forward(which, c, d):
        target = lax.rem(me + d, peers)
        return pltpu.make_async_remote_copy(
            src_ref=sends.at[which, target, pl.ds(c * rows, rows), :],
            dst_ref=recvs.at[which, own_lines(c), :],
            send_sem=fwd_s.at[which, c, d - 1], recv_sem=fwd_r.at[which, c, d - 1],
            device_id=(block, target), device_id_type=MESH,
        )

    def backward(which, c, d):
        target = lax.rem(me + d, peers)
        return pltpu.make_async_remote_copy(
            src_ref=backs.at[which, pl.ds((target * local_x + c * planes) * local_y, rows), :],
            dst_ref=homes.at[which, me, pl.ds(c * rows, rows), :],
            send_sem=bwd_s.at[which, c, d - 1], recv_sem=bwd_r.at[which, c, d - 1],
            device_id=(block, target), device_id_type=MESH,
        )

    barrier = pltpu.get_barrier_semaphore()
    pl.semaphore_signal(barrier, inc=1, device_id=(ahead, me), device_id_type=MESH)
    pl.semaphore_signal(barrier, inc=1, device_id=(behind, me), device_id_type=MESH)
    for d in range(1, peers):
        pl.semaphore_signal(
            barrier, inc=1, device_id=(block, lax.rem(me + d, peers)), device_id_type=MESH
        )
    pl.semaphore_wait(barrier, peers + 1)
    orb_in.wait()

    near_lead = min(3, chunks)
    far_lead = min(2, chunks)
    for c in range(near_lead):
        near_copy(c).start()
    tab_in.wait()

    def signed(index, length):
        return jnp.where(index < length // 2, index, index - length).astype(jnp.float32)

    freq_x = signed(lax.broadcasted_iota(jnp.int32, (width_x, width_z), 0), width_x)
    freq_z = signed(lax.broadcasted_iota(jnp.int32, (width_x, width_z), 1), width_z)
    square_xz = freq_x * freq_x + freq_z * freq_z
    scale = coulomb_scale / float(width_x * width_y * width_z)

    def weigh(j, carry):
        freq_y = signed(me * local_y + j, width_y)
        square = square_xz + freq_y * freq_y
        weight[j] = jnp.where(square > 0, scale / jnp.maximum(square, 1.0), 0.0)
        return carry

    lax.fori_loop(0, local_y, weigh, 0)

    def along_lanes(value):
        lead, rest = parts(value)
        return dot(jnp.concatenate([lead, rest], axis=1), tab[: 2 * width_z, :width_z]) + dot(
            lead, tab[:width_z, width_z:]
        )

    def along_rows(value):
        lead, rest = parts(value)
        length = value.shape[0]
        return dot(tab[2 * length :, :], jnp.concatenate([lead, rest], axis=0)) + dot(
            tab[:length, length:], lead
        )

    def transform_chunk(which, partner, c):
        span = pl.ds(c * planes, planes)
        density = (orb[span] * partner[span]).reshape(planes * width_y, width_z)
        density = along_lanes(density)
        result = along_rows(
            jnp.concatenate(
                [density[p * width_y : (p + 1) * width_y] for p in range(planes)], axis=1
            )
        )
        for p in range(planes):
            for g in range(peers):
                sends[which, g, pl.ds(c * rows + p * local_y, local_y), :] = result[
                    g * local_y : (g + 1) * local_y, p * width_z : (p + 1) * width_z
                ]
        for d in range(1, peers):
            forward(which, c, d).start()
        recvs[which, own_lines(c), :] = sends[which, me, pl.ds(c * rows, rows), :]

    def all_arrived(which):
        def arrived(c, carry):
            for d in range(1, peers):
                forward(which, c, d).wait_recv()
            return carry

        lax.fori_loop(0, chunks, arrived, 0)

    group = math.gcd(4, local_y)
    groups = local_y // group
    per_step = -(-groups // (chunks - half))

    def columns(which, s):
        lines = [pl.ds(s * group + u, width_x, stride=local_y) for u in range(group)]
        field = jnp.concatenate([recvs[which, line, :] for line in lines], axis=1)
        field = along_rows(field) * jnp.concatenate(
            [weight[s * group + u] for u in range(group)], axis=1
        )
        field = along_rows(field)
        for u in range(group):
            backs[which, lines[u], :] = field[:, u * width_z : (u + 1) * width_z]

    def send_back(which, c):
        for d in range(1, peers):
            backward(which, c, d).start()
        homes[which, me, pl.ds(c * rows, rows), :] = backs[which, own_lines(c), :]

    def potential(which, c):
        for d in range(1, peers):
            backward(which, c, d).wait_recv()
        stacked = jnp.concatenate(
            [
                jnp.concatenate(
                    [
                        homes[which, g, pl.ds(c * rows + p * local_y, local_y), :]
                        for g in range(peers)
                    ],
                    axis=0,
                )
                for p in range(planes)
            ],
            axis=1,
        )
        turned = along_rows(stacked)
        joined = jnp.concatenate(
            [turned[:, p * width_z : (p + 1) * width_z] for p in range(planes)], axis=0
        )
        return along_lanes(joined).reshape(planes, width_y, width_z)

    def apply_near(c):
        span = pl.ds(c * planes, planes)
        pot = potential(0, c)
        near_sum[span] = pot * orb[span]
        out[span] = -(pot * near[span])

    def apply_far(c):
        span = pl.ds(c * planes, planes)
        pot = potential(1, c)
        far_sum[span] = pot * orb[span]
        far_carry(c).start()
        out[span] = out[span] - pot * far[span]

    def near_in(c, carry):
        near_copy(c).wait_recv()

        @pl.when(c + near_lead < chunks)
        def _():
            near_copy(c + near_lead).start()

        @pl.when(c >= chunks - far_lead)
        def _():
            far_copy(c - (chunks - far_lead)).start()

        transform_chunk(0, near, c)
        return carry

    lax.fori_loop(0, chunks, near_in, 0)

    def far_in(c, carry):
        far_copy(c).wait_recv()

        @pl.when(c + far_lead < chunks)
        def _():
            far_copy(c + far_lead).start()

        transform_chunk(1, far, c)

        @pl.when(c == half)
        def _():
            all_arrived(0)

        @pl.when(c >= half)
        def _():
            for u in range(per_step):
                s = (c - half) * per_step + u

                @pl.when(s < groups)
                def _():
                    columns(0, s)

        return carry

    lax.fori_loop(0, chunks, far_in, 0)

    def back_first(c, carry):
        send_back(0, c)
        return carry

    lax.fori_loop(0, half, back_first, 0)
    all_arrived(1)

    def far_columns(s, carry):
        columns(1, s)
        return carry

    lax.fori_loop(0, groups, far_columns, 0)

    def back_both(c, carry):
        send_back(1, c)

        @pl.when(c + half < chunks)
        def _():
            send_back(0, c + half)

        return carry

    lax.fori_loop(0, chunks, back_both, 0)

    def apply_first(c, carry):
        apply_near(c)
        return carry

    lax.fori_loop(0, half, apply_first, 0)

    def outbound(s, carry):
        @pl.when(s < chunks)
        def _():
            apply_far(s)

        @pl.when(s + half < chunks)
        def _():
            apply_near(s + half)

        @pl.when((s > 0) & (s <= chunks))
        def _():
            c = s - 1
            span = pl.ds(c * planes, planes)
            far_carry(c).wait_recv()
            near_sum[span] = near_sum[span] + far_got[span]
            near_carry(c).start()

        @pl.when(s > 1)
        def _():
            c = s - 2
            span = pl.ds(c * planes, planes)
            near_carry(c).wait_recv()
            out[span] = out[span] - near_got[span]

        return carry

    lax.fori_loop(0, chunks + 2, outbound, 0)

    def drain(c, carry):
        near_copy(c).wait_send()
        far_copy(c).wait_send()
        far_carry(c).wait_send()
        near_carry(c).wait_send()
        for which in range(2):
            for d in range(1, peers):
                forward(which, c, d).wait_send()
                backward(which, c, d).wait_send()
        return carry

    lax.fori_loop(0, chunks, drain, 0)


def per_device(bands, peers, orbitals):
    _, local_x, width_y, width_z = orbitals.shape
    width_x = local_x * peers
    local_y = width_y // peers
    planes = math.gcd(4, local_x)
    chunks = local_x // planes
    slab = pltpu.VMEM((local_x, width_y, width_z), jnp.float32)
    by_peer = pltpu.VMEM((2, peers, local_x * local_y, width_z), jnp.float32)
    by_line = pltpu.VMEM((2, width_x * local_y, width_z), jnp.float32)
    dma = pltpu.SemaphoreType.DMA
    result = pl.pallas_call(
        functools.partial(kernel, bands, peers, planes),
        out_shape=jax.ShapeDtypeStruct((local_x, width_y, width_z), jnp.float32),
        in_specs=[pl.BlockSpec(memory_space=pl.ANY)] * 2,
        out_specs=pl.BlockSpec(memory_space=pltpu.VMEM),
        scratch_shapes=[slab, pltpu.VMEM((3 * width_z, 2 * width_z), jnp.bfloat16)]
        + [pltpu.VMEM((local_y, width_x, width_z), jnp.float32)]
        + [slab, slab, by_peer, by_line, by_line, by_peer, slab, slab, slab, slab]
        + [dma((2,))]
        + [dma((chunks,))] * 8
        + [dma((2, chunks, peers - 1))] * 4,
        compiler_params=pltpu.CompilerParams(
            collective_id=0, has_side_effects=True, vmem_limit_bytes=60 * 2**20
        ),
        name="exchange",
    )(orbitals[0], table(width_z))
    return result[None]


def solution(mesh):
    spec = P("band", "grid", None, None)
    body = functools.partial(per_device, mesh.shape["band"], mesh.shape["grid"])
    return jax.shard_map(body, mesh=mesh, in_specs=(spec,), out_specs=spec, check_vma=False)
```

time: 144 us -> 130 us (0.903)
  Pallas kernels: 137 us -> 126 us
  local copies, waits for them, and re-layouts: 6.75 us -> 3.14 us
    pallas_call x1, Pallas kernels: 137 us -> 126 us  [per_device(): pl.pallas_call(functools.partial(kernel, bands, peers, planes), out_shape...]
    unnamed x9 -> x1, local copies, waits for them, and re-layouts: 6.75 us -> 3.14 us
where the time goes in v1:
time: 130 us
  Pallas kernels  126 us (97%)
  local copies, waits for them, and re-layouts  3.14 us (2%)
    pallas_call x1, Pallas kernels, per_device(): pl.pallas_call(functools.partial(kernel, bands, peers, planes), out_shape...  126 us
    unnamed x1, local copies, waits for them, and re-layouts  3.14 us

profile of v1, /device:TPU:0, one launch (start us, length us, event | category | flops | bytes accessed | tf_op | source)
XLA Modules:
  0.0 129.5 jit_solution(12075956778515793401)
XLA Ops:
  0.0 126.4 %exchange.1 = f32[32,128,128]{2,1,0:T(8,128)} custom-call(f32[32,128,128]{2,1,0:T(8,128)} %bitcast.3, bf16[384,256]{1,0:T(8,128)(2,1)} %constant.2.clone.tab_hbm), custom_call_target="tpu_custom_call" | custom-call | tf_op jit(solution)/shard_map/exchange/pallas_call | solution.py:346
  126.4 3.1 %copy.4 = f32[1,32,128,128]{3,2,1,0:T(8,128)} copy(f32[1,32,128,128]{3,2,1,0:T(8,128)} %bitcast.2) | data formatting | bytes 4194304

commit v2 on v1

--- a/solution.py
+++ b/solution.py
@@ -34,7 +34,7 @@
 def kernel(
     bands, peers, planes,
     orb_hbm, tab_hbm, out,
-    orb, tab, weight, near, far, sends, recvs, backs, homes, far_sum, far_got, near_sum, near_got,
+    orb, tab, weight, partner, sends, recvs, backs, homes, sums, far_got, near_got,
     in_s, near_s, near_r, far_s, far_r, cfar_s, cfar_r, cnear_s, cnear_r, fwd_s, fwd_r, bwd_s, bwd_r,
 ):
     local_x, width_y, width_z = orb.shape
@@ -42,11 +42,14 @@
     local_y = width_y // peers
     chunks = local_x // planes
     rows = planes * local_y
-    half = chunks // 2
+    half = max(chunks // 2, 1)
     me = lax.axis_index("grid")
     block = lax.axis_index("band")
     ahead = lax.rem(block + 1, bands)
     behind = lax.rem(block + bands - 1, bands)
+    odd = lax.rem(block, 2)
+    near, far = partner.at[0], partner.at[1]
+    near_sum, far_sum = sums.at[0], sums.at[1]
 
     orb_in = pltpu.make_async_copy(orb_hbm, orb, in_s.at[0])
     tab_in = pltpu.make_async_copy(tab_hbm, tab, in_s.at[1])
@@ -139,9 +142,10 @@
             tab[:length, length:], lead
         )
 
-    def transform_chunk(which, partner, c):
+    def transform_chunk(which, c):
         span = pl.ds(c * planes, planes)
-        density = (orb[span] * partner[span]).reshape(planes * width_y, width_z)
+        other = partner[lax.rem(odd + which, 2), span]
+        density = (orb[span] * other).reshape(planes * width_y, width_z)
         density = along_lanes(density)
         result = along_rows(
             jnp.concatenate(
@@ -167,7 +171,7 @@
 
     group = math.gcd(4, local_y)
     groups = local_y // group
-    per_step = -(-groups // (chunks - half))
+    per_step = -(-groups // half)
 
     def columns(which, s):
         lines = [pl.ds(s * group + u, width_x, stride=local_y) for u in range(group)]
@@ -206,108 +210,130 @@
         )
         return along_lanes(joined).reshape(planes, width_y, width_z)
 
-    def apply_near(c):
+    def apply(which, c):
+        role = lax.rem(odd + which, 2)
         span = pl.ds(c * planes, planes)
-        pot = potential(0, c)
-        near_sum[span] = pot * orb[span]
-        out[span] = -(pot * near[span])
-
-    def apply_far(c):
-        span = pl.ds(c * planes, planes)
-        pot = potential(1, c)
-        far_sum[span] = pot * orb[span]
-        far_carry(c).start()
-        out[span] = out[span] - pot * far[span]
-
-    def near_in(c, carry):
-        near_copy(c).wait_recv()
-
-        @pl.when(c + near_lead < chunks)
-        def _():
-            near_copy(c + near_lead).start()
-
-        @pl.when(c >= chunks - far_lead)
-        def _():
-            far_copy(c - (chunks - far_lead)).start()
-
-        transform_chunk(0, near, c)
-        return carry
-
-    lax.fori_loop(0, chunks, near_in, 0)
-
-    def far_in(c, carry):
-        far_copy(c).wait_recv()
-
-        @pl.when(c + far_lead < chunks)
-        def _():
-            far_copy(c + far_lead).start()
-
-        transform_chunk(1, far, c)
-
-        @pl.when(c == half)
-        def _():
-            all_arrived(0)
-
-        @pl.when(c >= half)
-        def _():
-            for u in range(per_step):
-                s = (c - half) * per_step + u
-
-                @pl.when(s < groups)
-                def _():
-                    columns(0, s)
-
-        return carry
-
-    lax.fori_loop(0, chunks, far_in, 0)
-
-    def back_first(c, carry):
-        send_back(0, c)
-        return carry
-
-    lax.fori_loop(0, half, back_first, 0)
-    all_arrived(1)
-
-    def far_columns(s, carry):
-        columns(1, s)
-        return carry
-
-    lax.fori_loop(0, groups, far_columns, 0)
-
-    def back_both(c, carry):
-        send_back(1, c)
-
-        @pl.when(c + half < chunks)
-        def _():
-            send_back(0, c + half)
-
-        return carry
-
-    lax.fori_loop(0, chunks, back_both, 0)
-
-    def apply_first(c, carry):
-        apply_near(c)
-        return carry
-
-    lax.fori_loop(0, half, apply_first, 0)
-
-    def outbound(s, carry):
-        @pl.when(s < chunks)
-        def _():
-            apply_far(s)
-
-        @pl.when(s + half < chunks)
-        def _():
-            apply_near(s + half)
-
-        @pl.when((s > 0) & (s <= chunks))
-        def _():
-            c = s - 1
+        pot = potential(which, c)
+        sums[role, span] = pot * orb[span]
+        term = pot * partner[role, span]
+        if which == 0:
+            out[span] = -term
+        else:
+            out[span] = out[span] - term
+
+        @pl.when(role == 1)
+        def _():
+            far_carry(c).start()
+
+    def hand_on(which, c):
+        @pl.when(lax.rem(odd + which, 2) == 0)
+        def _():
             span = pl.ds(c * planes, planes)
             far_carry(c).wait_recv()
             near_sum[span] = near_sum[span] + far_got[span]
             near_carry(c).start()
 
+    def first_in(c, carry):
+        @pl.when(odd == 0)
+        def _():
+            near_copy(c).wait_recv()
+            far_copy(c).start()
+
+        @pl.when(c + near_lead < chunks)
+        def _():
+            near_copy(c + near_lead).start()
+
+        @pl.when((odd == 1) & (c >= chunks - far_lead))
+        def _():
+            near_copy(c - (chunks - far_lead)).wait_recv()
+            far_copy(c - (chunks - far_lead)).start()
+
+        @pl.when(odd == 1)
+        def _():
+            far_copy(c).wait_recv()
+
+        transform_chunk(0, c)
+        return carry
+
+    lax.fori_loop(0, chunks, first_in, 0)
+
+    def second_in(c, carry):
+        @pl.when((odd == 1) & (c + far_lead < chunks))
+        def _():
+            near_copy(c + far_lead).wait_recv()
+            far_copy(c + far_lead).start()
+
+        @pl.when(odd == 0)
+        def _():
+            far_copy(c).wait_recv()
+
+        transform_chunk(1, c)
+
+        @pl.when(c == chunks - half)
+        def _():
+            all_arrived(0)
+
+        @pl.when(c >= chunks - half)
+        def _():
+            for u in range(per_step):
+                s = (c - (chunks - half)) * per_step + u
+
+                @pl.when(s < groups)
+                def _():
+                    columns(0, s)
+
+        return carry
+
+    lax.fori_loop(0, chunks, second_in, 0)
+
+    def back_all(which):
+        def one(c, carry):
+            send_back(which, c)
+            return carry
+
+        lax.fori_loop(0, chunks, one, 0)
+
+    back_all(0)
+
+    def first_out(s, carry):
+        @pl.when(s < chunks)
+        def _():
+            apply(0, s)
+
+        @pl.when(s > 0)
+        def _():
+            hand_on(0, s - 1)
+
+        @pl.when(s == 0)
+        def _():
+            all_arrived(1)
+
+        @pl.when(s < half)
+        def _():
+            for u in range(per_step):
+                t = s * per_step + u
+
+                @pl.when(t < groups)
+                def _():
+                    columns(1, t)
+
+        @pl.when(s == half - 1)
+        def _():
+            back_all(1)
+
+        return carry
+
+    lax.fori_loop(0, chunks + 1, first_out, 0)
+
+    def second_out(s, carry):
+        @pl.when(s < chunks)
+        def _():
+            apply(1, s)
+
+        @pl.when((s > 0) & (s <= chunks))
+        def _():
+            hand_on(1, s - 1)
+
         @pl.when(s > 1)
         def _():
             c = s - 2
@@ -317,7 +343,7 @@
 
         return carry
 
-    lax.fori_loop(0, chunks + 2, outbound, 0)
+    lax.fori_loop(0, chunks + 2, second_out, 0)
 
     def drain(c, carry):
         near_copy(c).wait_send()
@@ -340,6 +366,7 @@
     planes = math.gcd(4, local_x)
     chunks = local_x // planes
     slab = pltpu.VMEM((local_x, width_y, width_z), jnp.float32)
+    slabs = pltpu.VMEM((2, local_x, width_y, width_z), jnp.float32)
     by_peer = pltpu.VMEM((2, peers, local_x * local_y, width_z), jnp.float32)
     by_line = pltpu.VMEM((2, width_x * local_y, width_z), jnp.float32)
     dma = pltpu.SemaphoreType.DMA
@@ -350,7 +377,7 @@
         out_specs=pl.BlockSpec(memory_space=pltpu.VMEM),
         scratch_shapes=[slab, pltpu.VMEM((3 * width_z, 2 * width_z), jnp.bfloat16)]
         + [pltpu.VMEM((local_y, width_x, width_z), jnp.float32)]
-        + [slab, slab, by_peer, by_line, by_line, by_peer, slab, slab, slab, slab]
+        + [slabs, by_peer, by_line, by_line, by_peer, slabs, slab, slab]
         + [dma((2,))]
         + [dma((chunks,))] * 8
         + [dma((2, chunks, peers - 1))] * 4,

time: 130 us -> 119 us (0.915)
  Pallas kernels: 126 us -> 116 us
    pallas_call x1, Pallas kernels: 126 us -> 116 us  [per_device(): pl.pallas_call(functools.partial(kernel, bands, peers, planes), out_shape...]
where the time goes in v2:
time: 119 us
  Pallas kernels  116 us (97%)
  local copies, waits for them, and re-layouts  3.14 us (3%)
    pallas_call x1, Pallas kernels, per_device(): pl.pallas_call(functools.partial(kernel, bands, peers, planes), out_shape...  116 us
    unnamed x1, local copies, waits for them, and re-layouts  3.14 us

profile of v2, /device:TPU:0, one launch (start us, length us, event | category | flops | bytes accessed | tf_op | source)
XLA Modules:
  0.0 119.1 jit_solution(11410448271335387189)
XLA Ops:
  0.0 116.0 %exchange.1 = f32[32,128,128]{2,1,0:T(8,128)} custom-call(f32[32,128,128]{2,1,0:T(8,128)} %bitcast.3, bf16[384,256]{1,0:T(8,128)(2,1)} %constant.2.clone.tab_hbm), custom_call_target="tpu_custom_call" | custom-call | tf_op jit(solution)/shard_map/exchange/pallas_call | solution.py:373
  116.0 3.1 %copy.4 = f32[1,32,128,128]{3,2,1,0:T(8,128)} copy(f32[1,32,128,128]{3,2,1,0:T(8,128)} %bitcast.2) | data formatting | bytes 4194304

commit v3 on v2

--- a/solution.py
+++ b/solution.py
@@ -33,9 +33,9 @@
 
 def kernel(
     bands, peers, planes,
-    orb_hbm, tab_hbm, out,
-    orb, tab, weight, partner, sends, recvs, backs, homes, sums, far_got, near_got,
-    in_s, near_s, near_r, far_s, far_r, cfar_s, cfar_r, cnear_s, cnear_r, fwd_s, fwd_r, bwd_s, bwd_r,
+    orb_hbm, tab_hbm, out_hbm,
+    out, orb, tab, weight, partner, sends, recvs, backs, homes, sums, far_got, near_got,
+    in_s, near_s, near_r, far_s, far_r, cfar_s, cfar_r, cnear_s, cnear_r, fwd_s, fwd_r, bwd_s, bwd_r, out_s,
 ):
     local_x, width_y, width_z = orb.shape
     width_x = local_x * peers
@@ -76,6 +76,10 @@
     def near_carry(c):
         return to_band(near_sum, near_got, c, cnear_s, cnear_r, behind)
 
+    def out_copy(c):
+        span = pl.ds(c * planes, planes)
+        return pltpu.make_async_copy(out.at[span], out_hbm.at[span], out_s.at[c])
+
     def own_lines(c):
         return pl.ds((me * local_x + c * planes) * local_y, rows)
 
@@ -107,8 +111,8 @@
     pl.semaphore_wait(barrier, peers + 1)
     orb_in.wait()
 
-    near_lead = min(3, chunks)
-    far_lead = min(2, chunks)
+    near_lead = min(4, chunks)
+    far_lead = min(3, chunks)
     for c in range(near_lead):
         near_copy(c).start()
     tab_in.wait()
@@ -340,6 +344,7 @@
             span = pl.ds(c * planes, planes)
             near_carry(c).wait_recv()
             out[span] = out[span] - near_got[span]
+            out_copy(c).start()
 
         return carry
 
@@ -350,6 +355,7 @@
         far_copy(c).wait_send()
         far_carry(c).wait_send()
         near_carry(c).wait_send()
+        out_copy(c).wait()
         for which in range(2):
             for d in range(1, peers):
                 forward(which, c, d).wait_send()
@@ -374,13 +380,14 @@
         functools.partial(kernel, bands, peers, planes),
         out_shape=jax.ShapeDtypeStruct((local_x, width_y, width_z), jnp.float32),
         in_specs=[pl.BlockSpec(memory_space=pl.ANY)] * 2,
-        out_specs=pl.BlockSpec(memory_space=pltpu.VMEM),
-        scratch_shapes=[slab, pltpu.VMEM((3 * width_z, 2 * width_z), jnp.bfloat16)]
+        out_specs=pl.BlockSpec(memory_space=pl.ANY),
+        scratch_shapes=[slab, slab, pltpu.VMEM((3 * width_z, 2 * width_z), jnp.bfloat16)]
         + [pltpu.VMEM((local_y, width_x, width_z), jnp.float32)]
         + [slabs, by_peer, by_line, by_line, by_peer, slabs, slab, slab]
         + [dma((2,))]
         + [dma((chunks,))] * 8
-        + [dma((2, chunks, peers - 1))] * 4,
+        + [dma((2, chunks, peers - 1))] * 4
+        + [dma((chunks,))],
         compiler_params=pltpu.CompilerParams(
             collective_id=0, has_side_effects=True, vmem_limit_bytes=60 * 2**20
         ),

time: 119 us -> 118 us (level)
    pallas_call x1, Pallas kernels: 116 us -> 115 us  [per_device(): pl.pallas_call(functools.partial(kernel, bands, peers, planes), out_shape...]
where the time goes in v3:
time: 118 us
  Pallas kernels  115 us (97%)
  local copies, waits for them, and re-layouts  3.14 us (3%)
    pallas_call x1, Pallas kernels, per_device(): pl.pallas_call(functools.partial(kernel, bands, peers, planes), out_shape...  115 us
    unnamed x1, local copies, waits for them, and re-layouts  3.14 us

profile of v3, /device:TPU:0, one launch (start us, length us, event | category | flops | bytes accessed | tf_op | source)
XLA Modules:
  0.0 117.8 jit_solution(10721557560661122682)
XLA Ops:
  0.0 114.7 %exchange.1 = f32[32,128,128]{2,1,0:T(8,128)} custom-call(f32[32,128,128]{2,1,0:T(8,128)} %bitcast.3, bf16[384,256]{1,0:T(8,128)(2,1)} %constant.2.clone.tab_hbm), custom_call_target="tpu_custom_call" | custom-call | tf_op jit(solution)/shard_map/exchange/pallas_call | solution.py:379
  114.7 3.1 %copy.4 = f32[1,32,128,128]{3,2,1,0:T(8,128)} copy(f32[1,32,128,128]{3,2,1,0:T(8,128)} %bitcast.2) | data formatting | bytes 4194304

commit v4 on v3

--- a/solution.py
+++ b/solution.py
@@ -308,20 +308,20 @@
         def _():
             hand_on(0, s - 1)
 
-        @pl.when(s == 0)
+        @pl.when(s == 1)
         def _():
             all_arrived(1)
 
-        @pl.when(s < half)
+        @pl.when((s > 0) & (s <= half))
         def _():
             for u in range(per_step):
-                t = s * per_step + u
+                t = (s - 1) * per_step + u
 
                 @pl.when(t < groups)
                 def _():
                     columns(1, t)
 
-        @pl.when(s == half - 1)
+        @pl.when(s == half)
         def _():
             back_all(1)
 

time: 118 us -> 118 us (level)
  no operation moved by 1% of the time
where the time goes in v4:
time: 118 us
  Pallas kernels  115 us (97%)
  local copies, waits for them, and re-layouts  3.14 us (3%)
    pallas_call x1, Pallas kernels, per_device(): pl.pallas_call(functools.partial(kernel, bands, peers, planes), out_shape...  115 us
    unnamed x1, local copies, waits for them, and re-layouts  3.14 us

profile of v4, /device:TPU:0, one launch (start us, length us, event | category | flops | bytes accessed | tf_op | source)
XLA Modules:
  0.0 117.8 jit_solution(16707476081569506494)
XLA Ops:
  0.0 114.7 %exchange.1 = f32[32,128,128]{2,1,0:T(8,128)} custom-call(f32[32,128,128]{2,1,0:T(8,128)} %bitcast.3, bf16[384,256]{1,0:T(8,128)(2,1)} %constant.2.clone.tab_hbm), custom_call_target="tpu_custom_call" | custom-call | tf_op jit(solution)/shard_map/exchange/pallas_call | solution.py:379
  114.7 3.1 %copy.4 = f32[1,32,128,128]{3,2,1,0:T(8,128)} copy(f32[1,32,128,128]{3,2,1,0:T(8,128)} %bitcast.2) | data formatting | bytes 4194304
